TPU v7x, 512 devices: a whole 4x4x16 slice. The times are simulated.
512 devices in a mesh: pm: 2 (over y_lo), ka: 128 (over x, z, core), isdf: 2 (over y_hi).
Axes of the slice: x: 4, y: 4 (y_hi: 2, y_lo: 2; y = y_hi * 2 + y_lo), z: 16, core: 2. Of those that a mesh axis runs over, the one named last changes fastest.
Arguments:
- amplitudes: bfloat16 [2, 2, 2, 256, 64, 256], P('pm', None, None, 'ka'), may hold values from -6 to 6
- conduction: bfloat16 [2, 256, 256, 512], P(None, 'ka', None, 'isdf'), may hold values from -0.375 to 0.375
- valence: bfloat16 [2, 256, 64, 512], P(None, 'ka'), may hold values from -0.75 to 0.75
- energy: float32 [256, 64, 256], P('ka', None, 'isdf'), may hold values from 0.5 to 2.5
- screened: bfloat16 [4, 2, 512, 512], P(None, None, 'isdf'), may hold values from -0.59765625 to 0.59765625
- coulomb: float32 [512, 512], P(None, 'isdf'), may hold values from -0.03125 to 0.03125
- mirror: int32 [256], P('ka'), may hold values from 0 to 255, as said below
- transfer_class: int32 [256, 256], P('ka'), may hold values from 0 to 3, as said below
Outputs:
- response: bfloat16 [2, 2, 2, 256, 64, 256], P('pm', None, None, 'ka', None, 'isdf')
Inputs may be any that keep to these rules, and one draw needn't show every extreme that they name: mirror[mirror[k]] = k; a k-point of block j (the aligned block of 2 k-points that holds it) has its mirror in block 127 - j. transfer_class[k, k2] depends only on (k - k2) mod 256.
All inputs are finite; a program needn't handle non-finite values.
Results may differ from a plain program's by a relative error of at most 0.015.
Values may be sent and summed in bfloat16 or wider, within the bound.
A program may use at most 128 MiB of HBM per device.

v0:
```python
import jax
import jax.numpy as jnp
from jax import lax
from jax.sharding import PartitionSpec as P

REACH = 2
HIGHEST = lax.Precision.HIGHEST


def swapped(block, axis, apart):
    count = lax.axis_size(axis)
    route = []
    for low in range(count):
        high = low | 1 << apart
        if high != low and high < count:
            route += [(low, high), (high, low)]
    return lax.ppermute(block, axis, route)


def shifted(value, axis, by):
    size = lax.axis_size(axis)
    return lax.ppermute(value, axis, [(i, (i + by) % size) for i in range(size)])


def pair_einsum(pattern, left, right, conjugate):

    def single(first, second):
        return jnp.einsum(pattern, first, second, preferred_element_type=jnp.float32)

    if conjugate:
        real_part = single(left[0], right[0]) + single(left[1], right[1])
        imag_part = single(left[1], right[0]) - single(left[0], right[1])
    else:
        real_part = single(left[0], right[0]) - single(left[1], right[1])
        imag_part = single(left[0], right[1]) + single(left[1], right[0])
    return (real_part, imag_part)


def conjugated(field):
    return jnp.stack([field[:, 0], -field[:, 1]], axis=1)


def coefficients(vector, conduction):
    real_part, imag_part = pair_einsum(
        "bkvc,kcm->bkvm", (vector[:, 0], vector[:, 1]), (conduction[0], conduction[1]), False
    )
    return jnp.stack([real_part, imag_part], axis=1).astype(jnp.bfloat16)


def amp_bits(field):
    for bit_number in range(lax.axis_size("ka").bit_length() - 1):
        field = swapped(field, "ka", bit_number)
    return field


def result_bits(field):
    for bit_number in range(lax.axis_size("ka").bit_length() - 1):
        field = swapped(field, "ka", bit_number)
    return field


def by_mirror(field, local_mirror):
    index = local_mirror[None, None, :, None, None]
    return jnp.where(index == 0, field[:, :, 0:1], field[:, :, 1:2])


def per_device(amplitudes, conduction, valence, energy, screened, coulomb, mirror, transfer_class):
    pm_index = lax.axis_index("pm")
    ka_index = lax.axis_index("ka")
    isdf_index = lax.axis_index("isdf")
    ka_count = lax.axis_size("ka")
    kpoint_count = conduction.shape[1]
    mu_count = conduction.shape[3]
    point_count = valence.shape[3]
    cond_share = energy.shape[2]
    vector_count = amplitudes.shape[1]
    is_plus = pm_index == 0
    parity = jnp.where(is_plus, 1.0, -1.0).astype(jnp.float32)
    exchange_weight = jnp.where(is_plus, 4.0, 0.0).astype(jnp.float32)
    local_amps = amplitudes[0]
    partner_amps = swapped(local_amps, "pm", 0)
    partner_side = jnp.where(is_plus, partner_amps, local_amps)
    distant_side = amp_bits(partner_side)
    direct = jnp.where(is_plus, local_amps, partner_amps).astype(jnp.float32)
    local_mirror = mirror - (ka_count - 1 - ka_index) * kpoint_count
    flipped = conjugated(by_mirror(distant_side, local_mirror).astype(jnp.float32))
    vector = (direct + parity * flipped).astype(jnp.bfloat16)
    own_coef = coefficients(vector, conduction)
    valence_part = lax.dynamic_slice_in_dim(valence, isdf_index * mu_count, mu_count, 3)
    rho_real = jnp.einsum(
        "kvm,bkvm->bm", valence_part[0], own_coef[:, 0], preferred_element_type=jnp.float32
    )
    rho_real = rho_real + jnp.einsum(
        "kvm,bkvm->bm", valence_part[1], own_coef[:, 1], preferred_element_type=jnp.float32
    )
    rho_imag = jnp.einsum(
        "kvm,bkvm->bm", valence_part[0], own_coef[:, 1], preferred_element_type=jnp.float32
    )
    rho_imag = rho_imag - jnp.einsum(
        "kvm,bkvm->bm", valence_part[1], own_coef[:, 0], preferred_element_type=jnp.float32
    )
    density = jnp.stack([rho_real, rho_imag], axis=1)
    spread = jnp.einsum("nm,brm->brn", coulomb, density, precision=HIGHEST)
    spread = lax.psum(spread, ("ka", "isdf"))
    potential = lax.dynamic_slice_in_dim(spread, isdf_index * mu_count, mu_count, 2)
    class_ids = jnp.arange(screened.shape[0], dtype=jnp.int32)

    def accumulate(totals, coef_block, valence_block, source):
        pair_real, pair_imag = pair_einsum(
            "bqvm,qvn->bqmn",
            (coef_block[:, 0], coef_block[:, 1]),
            (valence_block[0], valence_block[1]),
            True,
        )
        pair_real = pair_real.astype(jnp.bfloat16)
        pair_imag = pair_imag.astype(jnp.bfloat16)
        classes = lax.dynamic_slice_in_dim(transfer_class, source * kpoint_count, kpoint_count, 1)
        selector = (classes[:, :, None] == class_ids).astype(jnp.bfloat16)
        total_real, total_imag = totals
        for visitor in range(kpoint_count):
            chosen = jnp.einsum(
                "kw,wrmn->rkmn", selector[:, visitor], screened, preferred_element_type=jnp.float32
            ).astype(jnp.bfloat16)
            screen_real = chosen[0][None].astype(jnp.float32)
            screen_imag = chosen[1][None].astype(jnp.float32)
            visit_real = pair_real[:, visitor][:, None].astype(jnp.float32)
            visit_imag = pair_imag[:, visitor][:, None].astype(jnp.float32)
            total_real = total_real + (screen_real * visit_real - screen_imag * visit_imag)
            total_imag = total_imag + (screen_real * visit_imag + screen_imag * visit_real)
        return (total_real, total_imag)

    payload = (vector, conduction, valence)

    def advance(moving, offset):
        return shifted((moving[0], moving[1], moving[2]), "ka", offset)

    def unpack(moving):
        return (coefficients(moving[0], moving[1]), moving[2])

    def visit(totals, moving, distance):
        coef_block, valence_block = unpack(moving)
        source = jnp.mod(ka_index + distance, ka_count)
        return accumulate(totals, coef_block, valence_block, source)

    zero_field = jnp.zeros((vector_count, kpoint_count, mu_count, point_count), jnp.float32)
    totals = accumulate((zero_field, zero_field), own_coef, valence, ka_index)
    below_item = payload
    for count_done in range(REACH):
        below_item = advance(below_item, 1)
        totals = visit(totals, below_item, -(count_done + 1))
    above_item = payload
    for count_done in range(REACH):
        above_item = advance(above_item, -1)
        totals = visit(totals, above_item, count_done + 1)
    sum_real = totals[0].astype(jnp.bfloat16)
    sum_imag = totals[1].astype(jnp.bfloat16)
    back_real, back_imag = pair_einsum(
        "bkmn,kvn->bkvm", (sum_real, sum_imag), (valence[0], valence[1]), False
    )
    potential_real = potential[:, 0][:, None, None, :]
    potential_imag = potential[:, 1][:, None, None, :]
    exchange_real = potential_real * valence_part[0] - potential_imag * valence_part[1]
    exchange_imag = potential_real * valence_part[1] + potential_imag * valence_part[0]
    field_real = (exchange_weight * exchange_real - back_real).astype(jnp.bfloat16)
    field_imag = (exchange_weight * exchange_imag - back_imag).astype(jnp.bfloat16)
    out_real, out_imag = pair_einsum(
        "bkvm,kcm->bkvc", (field_real, field_imag), (conduction[0], conduction[1]), True
    )
    partial_out = jnp.stack([out_real, out_imag], axis=1)
    summed = lax.psum_scatter(
        partial_out.astype(jnp.bfloat16), "isdf", scatter_dimension=4, tiled=True
    ).astype(jnp.float32)
    vector_part = lax.dynamic_slice_in_dim(vector, isdf_index * cond_share, cond_share, 4).astype(
        jnp.float32
    )
    channel_out = (energy[None, None] * vector_part + summed).astype(jnp.bfloat16)
    partner_out = swapped(channel_out, "pm", 0)
    blended = (
        0.5 * (partner_out.astype(jnp.float32) + parity * channel_out.astype(jnp.float32))
    ).astype(jnp.bfloat16)
    distant_out = result_bits(blended)
    reflected = conjugated(by_mirror(distant_out, local_mirror))
    result = jnp.where(is_plus, blended, reflected)
    return result[None]


def solution(mesh):
    return jax.shard_map(
        per_device,
        mesh=mesh,
        in_specs=(
            P("pm", None, None, "ka", None, None),
            P(None, "ka", None, "isdf"),
            P(None, "ka", None, None),
            P("ka", None, "isdf"),
            P(None, None, "isdf", None),
            P(None, "isdf"),
            P("ka"),
            P("ka", None),
        ),
        out_specs=P("pm", None, None, "ka", None, "isdf"),
        check_vma=False,
    )
```

profile of v0, /device:TPU:2, one launch (start us, length us, event | category | flops | bytes accessed | tf_op | source)
XLA Modules:
  0.0 1086.2 jit_solution(11353441118219177994)
XLA Ops:
  8.6 10.8 collective-permute-start.15
  21.3 5.8 collective-permute-start.16
  28.1 3.5 collective-permute-start
  32.8 3.2 copy.48
  59.1 3.0 fusion.87
  66.2 3.5 fusion.75
  78.0 6.5 collective-permute-done.2
  88.5 12.3 %collective-permute-done.3 = bf16[2,2,2,64,256]{4,3,0,2,1:T(8,128)(2,1)S(1)} collective-permute-done((bf16[2,2,2,64,256]{4,3,0,2,1:T(8,128)(2,1)S(1)}, bf16[2,2,2,64,256]{4,3,0,2,1:T(8,128)(2,1)S(1)}, u32[]{:S(2)}, u32[]{:S(2)}) %collective-permute-start.3) | collective-permute-done | bytes 262176 | tf_op jit(solution)/shard_map/ppermute | solution.py:17
  105.3 22.7 %collective-permute-done.4 = bf16[2,2,2,64,256]{4,3,0,2,1:T(8,128)(2,1)S(1)} collective-permute-done((bf16[2,2,2,64,256]{4,3,0,2,1:T(8,128)(2,1)S(1)}, bf16[2,2,2,64,256]{4,3,0,2,1:T(8,128)(2,1)S(1)}, u32[]{:S(2)}, u32[]{:S(2)}) %collective-permute-start.4) | collective-permute-done | bytes 262176 | tf_op jit(solution)/shard_map/ppermute | solution.py:17
  128.0 14.7 %collective-permute-start.5 = (bf16[2,2,2,64,256]{4,3,0,2,1:T(8,128)(2,1)S(1)}, bf16[2,2,2,64,256]{4,3,0,2,1:T(8,128)(2,1)S(1)}, u32[]{:S(2)}, u32[]{:S(2)}) collective-permute-start(bf16[2,2,2,64,256]{4,3,0,2,1:T(8,128)(2,1)S(1)} %collective-permute-done.4), channel_id=1, source_target_pairs={{0,32},{32,0},{2,34},{34,2},{4,36},{36,4},{6,38},{38,6},{8,40},{40... | collective-permute-start | bytes 786440 | tf_op jit(solution)/shard_map/ppermute | solution.py:17
  144.7 14.9 %collective-permute-done.5 = bf16[2,2,2,64,256]{4,3,0,2,1:T(8,128)(2,1)S(1)} collective-permute-done((bf16[2,2,2,64,256]{4,3,0,2,1:T(8,128)(2,1)S(1)}, bf16[2,2,2,64,256]{4,3,0,2,1:T(8,128)(2,1)S(1)}, u32[]{:S(2)}, u32[]{:S(2)}) %collective-permute-start.5) | collective-permute-done | bytes 262176 | tf_op jit(solution)/shard_map/ppermute | solution.py:17
  164.4 5.4 collective-permute-done.6
  169.8 4.2 collective-permute-start.7
  200.1 5.8 collective-permute-start.19
  207.9 5.8 collective-permute-start.18
  225.0 583.0 %psum.7 = f32[2,2,512]{2,1,0:T(2,128)S(1)} all-reduce(f32[2,2,512]{2,1,0:T(2,128)S(1)} %fusion.90), channel_id=1, replica_groups=mesh['pm'=2,'ka'=128,'isdf'=2] {'ka','isdf'}, use_global_device_ids=true, to_apply=%region_0.1 | all-reduce | flops 2048 | bytes 16384 | tf_op jit(solution)/shard_map/psum | solution.py:104
  842.2 5.3 collective-permute-start.17
  875.2 9.2 add_convert_fusion
  884.5 9.5 add_convert_fusion.1
  898.4 92.4 %reduce-scatter.4.cloned.1.call-done = bf16[128,512]{1,0:T(8,128)(2,1)} async-done(((bf16[256,512]{1,0:T(8,128)(2,1)}), bf16[128,512]{1,0:T(8,128)(2,1)}) %reduce-scatter.4.cloned.1.call-update) | async-done | bytes 131088
  995.6 4.6 collective-permute-done.20
  1003.5 3.5 collective-permute-start.22
  1007.0 4.0 collective-permute-done.22
  1011.0 4.4 collective-permute-start.23
  1015.4 5.9 collective-permute-done.23
  1021.3 7.6 collective-permute-start.24
  1028.9 9.8 collective-permute-done.24
  1038.7 12.0 %collective-permute-start.25 = (bf16[2,2,2,64,128]{4,3,0,2,1:T(8,128)(2,1)S(1)}, bf16[2,2,2,64,128]{4,3,0,2,1:T(8,128)(2,1)S(1)}, u32[]{:S(2)}, u32[]{:S(2)}) collective-permute-start(bf16[2,2,2,64,128]{4,3,0,2,1:T(8,128)(2,1)S(1)} %collective-permute-done.24), channel_id=1, source_target_pairs={{0,32},{32,0},{2,34},{34,2},{4,36},{36,4},{6,38},{38,6},{8,40},{40... | collective-permute-start | bytes 393224 | tf_op jit(solution)/shard_map/ppermute | solution.py:17
  1050.8 12.1 %collective-permute-done.25 = bf16[2,2,2,64,128]{4,3,0,2,1:T(8,128)(2,1)S(1)} collective-permute-done((bf16[2,2,2,64,128]{4,3,0,2,1:T(8,128)(2,1)S(1)}, bf16[2,2,2,64,128]{4,3,0,2,1:T(8,128)(2,1)S(1)}, u32[]{:S(2)}, u32[]{:S(2)}) %collective-permute-start.25) | collective-permute-done | bytes 131104 | tf_op jit(solution)/shard_map/ppermute | solution.py:17
  1065.3 4.4 collective-permute-done.26
  1069.7 4.0 collective-permute-start.27
  1073.7 4.4 collective-permute-done.27
  (284 shorter events, 172.9 us)
Async XLA Ops:
  6.5 218.0 %copy-start = (f32[512,256]{1,0:T(8,128)S(1)}, f32[512,256]{1,0:T(8,128)}, u32[]{:S(2)}) copy-start(f32[512,256]{1,0:T(8,128)} %param.13) | copy-start | bytes 1572868
  6.5 984.3 %reduce-scatter.4.cloned.1.call-start = ((), (), s32[]{:S(2)}) async-start(), calls=%async_computation.1 | async-start | bytes 393216
  6.5 199.4 %collective-permute-start.9 = (bf16[2,2,256,256]{3,2,1,0:T(8,128)(2,1)}, bf16[2,2,256,256]{3,2,1,0:T(8,128)(2,1)}, u32[]{:S(2)}, u32[]{:S(2)}) collective-permute-start(bf16[2,2,256,256]{3,2,1,0:T(8,128)(2,1)} %param.9), channel_id=1, source_target_pairs={{0,2},{2,4},{4,6},{6,8},{8,10},{10,12},{12,14},{14,16},{16,18},{18... | collective-permute-start | bytes 1572872 | tf_op jit(solution)/shard_map/ppermute | solution.py:22
  8.6 199.3 %collective-permute-start.15 = (bf16[2,2,256,256]{3,2,1,0:T(8,128)(2,1)}, bf16[2,2,256,256]{3,2,1,0:T(8,128)(2,1)}, u32[]{:S(2)}, u32[]{:S(2)}) collective-permute-start(bf16[2,2,256,256]{3,2,1,0:T(8,128)(2,1)} %param.9), channel_id=1, source_target_pairs={{0,254},{2,0},{4,2},{6,4},{8,6},{10,8},{12,10},{14,12},{16,14},{18... | collective-permute-start | bytes 1572872 | tf_op jit(solution)/shard_map/ppermute | solution.py:22
  19.4 178.6 %collective-permute-start.10 = (bf16[2,2,64,512]{3,2,1,0:T(8,128)(2,1)}, bf16[2,2,64,512]{3,2,1,0:T(8,128)(2,1)}, u32[]{:S(2)}, u32[]{:S(2)}) collective-permute-start(bf16[2,2,64,512]{3,2,1,0:T(8,128)(2,1)} %param.10), channel_id=1, source_target_pairs={{0,2},{2,4},{4,6},{6,8},{8,10},{10,12},{12,14},{14,16},{16,18},{18... | collective-permute-start | bytes 786440 | tf_op jit(solution)/shard_map/ppermute | solution.py:22
  21.3 178.8 %collective-permute-start.16 = (bf16[2,2,64,512]{3,2,1,0:T(8,128)(2,1)}, bf16[2,2,64,512]{3,2,1,0:T(8,128)(2,1)}, u32[]{:S(2)}, u32[]{:S(2)}) collective-permute-start(bf16[2,2,64,512]{3,2,1,0:T(8,128)(2,1)} %param.10), channel_id=1, source_target_pairs={{0,254},{2,0},{4,2},{6,4},{8,6},{10,8},{12,10},{14,12},{16,14},{18... | collective-permute-start | bytes 786440 | tf_op jit(solution)/shard_map/ppermute | solution.py:22
  28.1 41.6 %collective-permute-start = (bf16[2,2,2,64,256]{4,3,0,2,1:T(8,128)(2,1)S(1)}, bf16[2,2,2,64,256]{4,3,0,2,1:T(8,128)(2,1)S(1)}, u32[]{:S(2)}, u32[]{:S(2)}) collective-permute-start(bf16[2,2,2,64,256]{4,3,0,2,1:T(8,128)(2,1)S(1)} %bitcast.655), channel_id=1, source_target_pairs={{0,256},{256,0},{1,257},{257,1},{2,258},{258,2},{3,259},{259,3},{4... | collective-permute-start | bytes 786440 | tf_op jit(solution)/shard_map/ppermute | solution.py:17
  69.7 4.1 collective-permute-start.1
  73.9 10.7 collective-permute-start.2
  84.6 16.3 %collective-permute-start.3 = (bf16[2,2,2,64,256]{4,3,0,2,1:T(8,128)(2,1)S(1)}, bf16[2,2,2,64,256]{4,3,0,2,1:T(8,128)(2,1)S(1)}, u32[]{:S(2)}, u32[]{:S(2)}) collective-permute-start(bf16[2,2,2,64,256]{4,3,0,2,1:T(8,128)(2,1)S(1)} %collective-permute-done.2), channel_id=1, source_target_pairs={{0,8},{8,0},{2,10},{10,2},{4,12},{12,4},{6,14},{14,6},{16,24},{24,... | collective-permute-start | bytes 786440 | tf_op jit(solution)/shard_map/ppermute | solution.py:17
  100.8 27.1 %collective-permute-start.4 = (bf16[2,2,2,64,256]{4,3,0,2,1:T(8,128)(2,1)S(1)}, bf16[2,2,2,64,256]{4,3,0,2,1:T(8,128)(2,1)S(1)}, u32[]{:S(2)}, u32[]{:S(2)}) collective-permute-start(bf16[2,2,2,64,256]{4,3,0,2,1:T(8,128)(2,1)S(1)} %collective-permute-done.3), channel_id=1, source_target_pairs={{0,16},{16,0},{2,18},{18,2},{4,20},{20,4},{6,22},{22,6},{8,24},{24... | collective-permute-start | bytes 786440 | tf_op jit(solution)/shard_map/ppermute | solution.py:17
  128.0 31.6 %collective-permute-start.5 = (bf16[2,2,2,64,256]{4,3,0,2,1:T(8,128)(2,1)S(1)}, bf16[2,2,2,64,256]{4,3,0,2,1:T(8,128)(2,1)S(1)}, u32[]{:S(2)}, u32[]{:S(2)}) collective-permute-start(bf16[2,2,2,64,256]{4,3,0,2,1:T(8,128)(2,1)S(1)} %collective-permute-done.4), channel_id=1, source_target_pairs={{0,32},{32,0},{2,34},{34,2},{4,36},{36,4},{6,38},{38,6},{8,40},{40... | collective-permute-start | bytes 786440 | tf_op jit(solution)/shard_map/ppermute | solution.py:17
  159.6 10.2 collective-permute-start.6
  169.8 43.8 %collective-permute-start.7 = (bf16[2,2,2,64,256]{4,3,0,2,1:T(8,128)(2,1)}, bf16[2,2,2,64,256]{4,3,0,2,1:T(8,128)(2,1)}, u32[]{:S(2)}, u32[]{:S(2)}) collective-permute-start(bf16[2,2,2,64,256]{4,3,0,2,1:T(8,128)(2,1)} %collective-permute-done.6), channel_id=1, source_target_pairs={{0,128},{128,0},{2,130},{130,2},{4,132},{132,4},{6,134},{134,6},{8... | collective-permute-start | bytes 786440 | tf_op jit(solution)/shard_map/ppermute | solution.py:17
  198.1 654.0 %collective-permute-start.13 = (bf16[2,2,64,512]{3,2,1,0:T(8,128)(2,1)}, bf16[2,2,64,512]{3,2,1,0:T(8,128)(2,1)}, u32[]{:S(2)}, u32[]{:S(2)}) collective-permute-start(bf16[2,2,64,512]{3,2,1,0:T(8,128)(2,1)} %collective-permute-done.10), channel_id=1, source_target_pairs={{0,2},{2,4},{4,6},{6,8},{8,10},{10,12},{12,14},{14,16},{16,18},{18... | collective-permute-start | bytes 786440 | tf_op jit(solution)/shard_map/ppermute | solution.py:22
  200.1 664.4 %collective-permute-start.19 = (bf16[2,2,64,512]{3,2,1,0:T(8,128)(2,1)}, bf16[2,2,64,512]{3,2,1,0:T(8,128)(2,1)}, u32[]{:S(2)}, u32[]{:S(2)}) collective-permute-start(bf16[2,2,64,512]{3,2,1,0:T(8,128)(2,1)} %collective-permute-done.16), channel_id=1, source_target_pairs={{0,254},{2,0},{4,2},{6,4},{8,6},{10,8},{12,10},{14,12},{16,14},{18... | collective-permute-start | bytes 786440 | tf_op jit(solution)/shard_map/ppermute | solution.py:22
  205.9 636.3 %collective-permute-start.12 = (bf16[2,2,256,256]{3,2,1,0:T(8,128)(2,1)}, bf16[2,2,256,256]{3,2,1,0:T(8,128)(2,1)}, u32[]{:S(2)}, u32[]{:S(2)}) collective-permute-start(bf16[2,2,256,256]{3,2,1,0:T(8,128)(2,1)} %collective-permute-done.9), channel_id=1, source_target_pairs={{0,2},{2,4},{4,6},{6,8},{8,10},{10,12},{12,14},{14,16},{16,18},{18... | collective-permute-start | bytes 1572872 | tf_op jit(solution)/shard_map/ppermute | solution.py:22
  207.9 652.0 %collective-permute-start.18 = (bf16[2,2,256,256]{3,2,1,0:T(8,128)(2,1)}, bf16[2,2,256,256]{3,2,1,0:T(8,128)(2,1)}, u32[]{:S(2)}, u32[]{:S(2)}) collective-permute-start(bf16[2,2,256,256]{3,2,1,0:T(8,128)(2,1)} %collective-permute-done.15), channel_id=1, source_target_pairs={{0,254},{2,0},{4,2},{6,4},{8,6},{10,8},{12,10},{14,12},{16,14},{18... | collective-permute-start | bytes 1572872 | tf_op jit(solution)/shard_map/ppermute | solution.py:22
  217.9 594.7 %collective-permute-start.8 = (bf16[2,2,2,64,256]{4,3,0,2,1:T(8,128)(2,1)}, bf16[2,2,2,64,256]{4,3,0,2,1:T(8,128)(2,1)}, u32[]{:S(2)}, u32[]{:S(2)}) collective-permute-start(bf16[2,2,2,64,256]{4,3,0,2,1:T(8,128)(2,1)} %fusion.89), channel_id=1, source_target_pairs={{0,2},{2,4},{4,6},{6,8},{8,10},{10,12},{12,14},{14,16},{16,18},{18... | collective-permute-start | bytes 786440 | tf_op jit(solution)/shard_map/ppermute | solution.py:22
  225.0 584.7 %copy-start.46 = (bf16[2,2,64,256]{3,2,1,0:T(8,128)(2,1)S(1)}, bf16[2,2,64,256]{3,2,1,0:T(8,128)(2,1)}, u32[]{:S(2)}) copy-start(bf16[2,2,64,256]{3,2,1,0:T(8,128)(2,1)} %get-tuple-element.68) | copy-start | bytes 393220
  812.6 14.6 %collective-permute-start.14 = (bf16[2,2,2,64,256]{4,3,0,2,1:T(8,128)(2,1)}, bf16[2,2,2,64,256]{4,3,0,2,1:T(8,128)(2,1)S(1)}, u32[]{:S(2)}, u32[]{:S(2)}) collective-permute-start(bf16[2,2,2,64,256]{4,3,0,2,1:T(8,128)(2,1)} %fusion.89), channel_id=1, source_target_pairs={{0,254},{2,0},{4,2},{6,4},{8,6},{10,8},{12,10},{14,12},{16,14},{18... | collective-permute-start | bytes 786440 | tf_op jit(solution)/shard_map/ppermute | solution.py:22
  827.2 20.3 %collective-permute-start.11 = (bf16[2,2,2,64,256]{4,3,0,2,1:T(8,128)(2,1)}, bf16[2,2,2,64,256]{4,3,0,2,1:T(8,128)(2,1)S(1)}, u32[]{:S(2)}, u32[]{:S(2)}) collective-permute-start(bf16[2,2,2,64,256]{4,3,0,2,1:T(8,128)(2,1)} %collective-permute-done.8), channel_id=1, source_target_pairs={{0,2},{2,4},{4,6},{6,8},{8,10},{10,12},{12,14},{14,16},{16,18},{18... | collective-permute-start | bytes 786440 | tf_op jit(solution)/shard_map/ppermute | solution.py:22
  842.2 17.7 %collective-permute-start.17 = (bf16[2,2,2,64,256]{4,3,0,2,1:T(8,128)(2,1)S(1)}, bf16[2,2,2,64,256]{4,3,0,2,1:T(8,128)(2,1)S(1)}, u32[]{:S(2)}, u32[]{:S(2)}) collective-permute-start(bf16[2,2,2,64,256]{4,3,0,2,1:T(8,128)(2,1)S(1)} %collective-permute-done.14), channel_id=1, source_target_pairs={{0,254},{2,0},{4,2},{6,4},{8,6},{10,8},{12,10},{14,12},{16,14},{18... | collective-permute-start | bytes 786440 | tf_op jit(solution)/shard_map/ppermute | solution.py:22
  896.9 182.0 %copy-start.1 = (f32[512,256]{1,0:T(8,128)S(1)}, f32[512,256]{1,0:T(8,128)}, u32[]{:S(2)}) copy-start(f32[512,256]{1,0:T(8,128)} %param.13) | copy-start | bytes 1572868
  993.1 7.1 collective-permute-start.20
  1000.3 3.2 collective-permute-start.21
  1003.5 7.4 collective-permute-start.22
  1011.0 10.3 collective-permute-start.23
  1021.3 17.5 %collective-permute-start.24 = (bf16[2,2,2,64,128]{4,3,0,2,1:T(8,128)(2,1)S(1)}, bf16[2,2,2,64,128]{4,3,0,2,1:T(8,128)(2,1)S(1)}, u32[]{:S(2)}, u32[]{:S(2)}) collective-permute-start(bf16[2,2,2,64,128]{4,3,0,2,1:T(8,128)(2,1)S(1)} %collective-permute-done.23), channel_id=1, source_target_pairs={{0,16},{16,0},{2,18},{18,2},{4,20},{20,4},{6,22},{22,6},{8,24},{24... | collective-permute-start | bytes 393224 | tf_op jit(solution)/shard_map/ppermute | solution.py:17
  1038.7 24.1 %collective-permute-start.25 = (bf16[2,2,2,64,128]{4,3,0,2,1:T(8,128)(2,1)S(1)}, bf16[2,2,2,64,128]{4,3,0,2,1:T(8,128)(2,1)S(1)}, u32[]{:S(2)}, u32[]{:S(2)}) collective-permute-start(bf16[2,2,2,64,128]{4,3,0,2,1:T(8,128)(2,1)S(1)} %collective-permute-done.24), channel_id=1, source_target_pairs={{0,32},{32,0},{2,34},{34,2},{4,36},{36,4},{6,38},{38,6},{8,40},{40... | collective-permute-start | bytes 393224 | tf_op jit(solution)/shard_map/ppermute | solution.py:17
  1062.9 6.8 collective-permute-start.26
  1069.7 8.4 collective-permute-start.27
  (58 other events, 577.1 us)
Sparse Core Ops, SparseCore 0:
  898.5 92.2 reduce-scatter.3
where the time goes:
time: 1100 us; the launch traced here: 1090 us
  blocking collectives  583 us (53%)
  waiting for transfers between devices  201 us (18%)
  starting transfers between devices  120 us (11%)
  matrix products  76.3 us (7%)
  other arithmetic  56 us (5%)
  local copies, waits for them, and re-layouts  35.4 us (3%)
  between operations  15.1 us (1%)
    psum x1, blocking collectives, per_device(): spread = lax.psum(spread, ('ka', 'isdf'))  583 us
    ppermute x16, waiting for transfers between devices, swapped(): return lax.ppermute(block, axis, route)  108 us
    unnamed x2, waiting for transfers between devices  92.5 us
    ppermute x16, starting transfers between devices, swapped(): return lax.ppermute(block, axis, route)  71.9 us
    dot_general x48, matrix products, single(): jnp.einsum(pattern, first, second, preferred_element_type=jnp.float32)  53.4 us
    ppermute x12, starting transfers between devices, shifted(): lax.ppermute(value, axis, [(i, (i + by) % size) for i in range(size)])  47.7 us
    mul x10, other arithmetic, accumulate(): screen_real * visit_real - screen_imag * visit_imag  23 us
    dot_general x10, matrix products, accumulate(): jnp.einsum('kw,wrmn->rkmn', selector[:, visitor], screened, preferred_ele...  22.4 us
  transfers between devices with their start and end apart: 29, of which 14 were waited for; matrix products, arithmetic and copies ran while one was open for 12% of the time, Pallas kernels for 0%

commit v1 on v0

--- a/solution.py
+++ b/solution.py
@@ -101,7 +101,8 @@
     )
     density = jnp.stack([rho_real, rho_imag], axis=1)
     spread = jnp.einsum("nm,brm->brn", coulomb, density, precision=HIGHEST)
-    spread = lax.psum(spread, ("ka", "isdf"))
+    for over in ("ka", "isdf"):
+        spread = lax.psum(spread, over)
     potential = lax.dynamic_slice_in_dim(spread, isdf_index * mu_count, mu_count, 2)
     class_ids = jnp.arange(screened.shape[0], dtype=jnp.int32)
 

time: 1100 us -> 700 us (0.64)
  the two profiles are of different devices: /device:TPU:2 before, /device:TPU:4 now
where the time goes in v1:
time: 700 us; the launch traced here: 690 us
  blocking collectives  223 us (32%)
  waiting for transfers between devices  167 us (24%)
  starting transfers between devices  118 us (17%)
  matrix products  76.2 us (11%)
  other arithmetic  55.9 us (8%)
  local copies, waits for them, and re-layouts  35.3 us (5%)
  between operations  15.1 us (2%)
    psum x2, blocking collectives, per_device(): spread = lax.psum(spread, over)  223 us
    ppermute x16, waiting for transfers between devices, swapped(): return lax.ppermute(block, axis, route)  109 us
    ppermute x16, starting transfers between devices, swapped(): return lax.ppermute(block, axis, route)  69.9 us
    unnamed x2, waiting for transfers between devices  57.9 us
    dot_general x48, matrix products, single(): jnp.einsum(pattern, first, second, preferred_element_type=jnp.float32)  53.4 us
    ppermute x12, starting transfers between devices, shifted(): lax.ppermute(value, axis, [(i, (i + by) % size) for i in range(size)])  47.7 us
    mul x10, other arithmetic, accumulate(): screen_real * visit_real - screen_imag * visit_imag  22.9 us
    dot_general x10, matrix products, accumulate(): jnp.einsum('kw,wrmn->rkmn', selector[:, visitor], screened, preferred_ele...  22.4 us
  transfers between devices with their start and end apart: 29, of which 14 were waited for; matrix products, arithmetic and copies ran while one was open for 19% of the time, Pallas kernels for 0%

profile of v1, /device:TPU:4, one launch (start us, length us, event | category | flops | bytes accessed | tf_op | source)
XLA Modules:
  0.0 689.6 jit_solution(9333920358687279829)
XLA Ops:
  8.6 10.8 %collective-permute-start.15 = (bf16[2,2,256,256]{3,2,1,0:T(8,128)(2,1)}, bf16[2,2,256,256]{3,2,1,0:T(8,128)(2,1)}, u32[]{:S(2)}, u32[]{:S(2)}) collective-permute-start(bf16[2,2,256,256]{3,2,1,0:T(8,128)(2,1)} %param.9), channel_id=1, source_target_pairs={{0,254},{2,0},{4,2},{6,4},{8,6},{10,8},{12,10},{14,12},{16,14},{18... | collective-permute-start | bytes 1572872 | tf_op jit(solution)/shard_map/ppermute | solution.py:22
  21.3 5.8 collective-permute-start.16
  28.1 3.5 collective-permute-start
  32.7 3.2 copy.48
  59.0 3.0 fusion.87
  66.1 3.5 fusion.75
  77.9 6.5 collective-permute-done.2
  88.5 12.3 %collective-permute-done.3 = bf16[2,2,2,64,256]{4,3,0,2,1:T(8,128)(2,1)S(1)} collective-permute-done((bf16[2,2,2,64,256]{4,3,0,2,1:T(8,128)(2,1)S(1)}, bf16[2,2,2,64,256]{4,3,0,2,1:T(8,128)(2,1)S(1)}, u32[]{:S(2)}, u32[]{:S(2)}) %collective-permute-start.3) | collective-permute-done | bytes 262176 | tf_op jit(solution)/shard_map/ppermute | solution.py:17
  105.3 22.6 %collective-permute-done.4 = bf16[2,2,2,64,256]{4,3,0,2,1:T(8,128)(2,1)S(1)} collective-permute-done((bf16[2,2,2,64,256]{4,3,0,2,1:T(8,128)(2,1)S(1)}, bf16[2,2,2,64,256]{4,3,0,2,1:T(8,128)(2,1)S(1)}, u32[]{:S(2)}, u32[]{:S(2)}) %collective-permute-start.4) | collective-permute-done | bytes 262176 | tf_op jit(solution)/shard_map/ppermute | solution.py:17
  127.9 14.7 %collective-permute-start.5 = (bf16[2,2,2,64,256]{4,3,0,2,1:T(8,128)(2,1)S(1)}, bf16[2,2,2,64,256]{4,3,0,2,1:T(8,128)(2,1)S(1)}, u32[]{:S(2)}, u32[]{:S(2)}) collective-permute-start(bf16[2,2,2,64,256]{4,3,0,2,1:T(8,128)(2,1)S(1)} %collective-permute-done.4), channel_id=1, source_target_pairs={{0,32},{32,0},{2,34},{34,2},{4,36},{36,4},{6,38},{38,6},{8,40},{40... | collective-permute-start | bytes 786440 | tf_op jit(solution)/shard_map/ppermute | solution.py:17
  144.7 14.9 %collective-permute-done.5 = bf16[2,2,2,64,256]{4,3,0,2,1:T(8,128)(2,1)S(1)} collective-permute-done((bf16[2,2,2,64,256]{4,3,0,2,1:T(8,128)(2,1)S(1)}, bf16[2,2,2,64,256]{4,3,0,2,1:T(8,128)(2,1)S(1)}, u32[]{:S(2)}, u32[]{:S(2)}) %collective-permute-start.5) | collective-permute-done | bytes 262176 | tf_op jit(solution)/shard_map/ppermute | solution.py:17
  159.6 3.1 collective-permute-start.6
  164.7 5.0 collective-permute-done.6
  198.6 5.8 collective-permute-start.19
  206.4 5.8 collective-permute-start.18
  223.5 216.0 %psum.14 = f32[2,2,512]{2,1,0:T(2,128)S(1)} all-reduce(f32[2,2,512]{2,1,0:T(2,128)S(1)} %fusion.90), channel_id=1, replica_groups=mesh['pm'=2,'ka'=128,'isdf'=2] {'ka'}, use_global_device_ids=true, to_apply=%region_0.1 | all-reduce | flops 2048 | bytes 16384 | tf_op jit(solution)/shard_map/psum | solution.py:105
  439.5 6.5 psum.15
  480.2 5.3 collective-permute-start.17
  513.2 9.2 %add_convert_fusion = bf16[2,2,256,512]{3,2,0,1:T(8,128)(2,1)S(1)} fusion(f32[2,256,512]{2,1,0:T(8,128)} %get-tuple-element.46, f32[2,256,512]{2,1,0:T(8,128)S(1)} %copy-done.19, f32[2,256,512]{2,1,0:T(8,128)} %get-tuple-element.71, f32[2,256,512]{2,1,0:T(8,128)S(1)} %copy-done.18, f32[2,256,512]{2,1,0:T(8,128)} %get-tuple-element.45, ...), kind=kLoop, calls=%fused_computation | loop fusion | flops 20971520 | bytes 42991616 | tf_op jit(solution)/shard_map/convert_element_type | solution.py:157
  522.4 9.5 %add_convert_fusion.1 = bf16[2,2,256,512]{3,2,0,1:T(8,128)(2,1)S(1)} fusion(f32[2,256,512]{2,1,0:T(8,128)} %get-tuple-element.46, f32[2,256,512]{2,1,0:T(8,128)S(1)} %copy-done.19, f32[2,256,512]{2,1,0:T(8,128)} %get-tuple-element.71, f32[2,256,512]{2,1,0:T(8,128)S(1)} %copy-done.18, f32[2,256,512]{2,1,0:T(8,128)} %get-tuple-element.45, ...), kind=kLoop, calls=%fused_computation.1 | loop fusion | flops 20971520 | bytes 42991616 | tf_op jit(solution)/shard_map/convert_element_type | solution.py:156
  536.3 57.9 %reduce-scatter.4.cloned.1.call-done = bf16[128,512]{1,0:T(8,128)(2,1)} async-done(((bf16[256,512]{1,0:T(8,128)(2,1)}), bf16[128,512]{1,0:T(8,128)(2,1)}) %reduce-scatter.4.cloned.1.call-update) | async-done | bytes 131088
  599.0 4.6 collective-permute-done.20
  606.9 3.5 collective-permute-start.22
  610.4 4.0 collective-permute-done.22
  614.4 4.4 collective-permute-start.23
  618.8 5.9 collective-permute-done.23
  624.7 7.7 %collective-permute-start.24 = (bf16[2,2,2,64,128]{4,3,0,2,1:T(8,128)(2,1)S(1)}, bf16[2,2,2,64,128]{4,3,0,2,1:T(8,128)(2,1)S(1)}, u32[]{:S(2)}, u32[]{:S(2)}) collective-permute-start(bf16[2,2,2,64,128]{4,3,0,2,1:T(8,128)(2,1)S(1)} %collective-permute-done.23), channel_id=1, source_target_pairs={{0,16},{16,0},{2,18},{18,2},{4,20},{20,4},{6,22},{22,6},{8,24},{24... | collective-permute-start | bytes 393224 | tf_op jit(solution)/shard_map/ppermute | solution.py:17
  632.3 9.9 %collective-permute-done.24 = bf16[2,2,2,64,128]{4,3,0,2,1:T(8,128)(2,1)S(1)} collective-permute-done((bf16[2,2,2,64,128]{4,3,0,2,1:T(8,128)(2,1)S(1)}, bf16[2,2,2,64,128]{4,3,0,2,1:T(8,128)(2,1)S(1)}, u32[]{:S(2)}, u32[]{:S(2)}) %collective-permute-start.24) | collective-permute-done | bytes 131104 | tf_op jit(solution)/shard_map/ppermute | solution.py:17
  642.2 12.0 %collective-permute-start.25 = (bf16[2,2,2,64,128]{4,3,0,2,1:T(8,128)(2,1)S(1)}, bf16[2,2,2,64,128]{4,3,0,2,1:T(8,128)(2,1)S(1)}, u32[]{:S(2)}, u32[]{:S(2)}) collective-permute-start(bf16[2,2,2,64,128]{4,3,0,2,1:T(8,128)(2,1)S(1)} %collective-permute-done.24), channel_id=1, source_target_pairs={{0,32},{32,0},{2,34},{34,2},{4,36},{36,4},{6,38},{38,6},{8,40},{40... | collective-permute-start | bytes 393224 | tf_op jit(solution)/shard_map/ppermute | solution.py:17
  654.2 12.1 %collective-permute-done.25 = bf16[2,2,2,64,128]{4,3,0,2,1:T(8,128)(2,1)S(1)} collective-permute-done((bf16[2,2,2,64,128]{4,3,0,2,1:T(8,128)(2,1)S(1)}, bf16[2,2,2,64,128]{4,3,0,2,1:T(8,128)(2,1)S(1)}, u32[]{:S(2)}, u32[]{:S(2)}) %collective-permute-start.25) | collective-permute-done | bytes 131104 | tf_op jit(solution)/shard_map/ppermute | solution.py:17
  669.3 3.9 collective-permute-done.26
  675.5 6.0 collective-permute-done.27
  (285 shorter events, 175.7 us)
Async XLA Ops:
  6.5 216.4 %copy-start = (f32[512,256]{1,0:T(8,128)S(1)}, f32[512,256]{1,0:T(8,128)}, u32[]{:S(2)}) copy-start(f32[512,256]{1,0:T(8,128)} %param.13) | copy-start | bytes 1572868
  6.5 587.7 %reduce-scatter.4.cloned.1.call-start = ((), (), s32[]{:S(2)}) async-start(), calls=%async_computation.1 | async-start | bytes 393216
  6.5 197.9 %collective-permute-start.9 = (bf16[2,2,256,256]{3,2,1,0:T(8,128)(2,1)}, bf16[2,2,256,256]{3,2,1,0:T(8,128)(2,1)}, u32[]{:S(2)}, u32[]{:S(2)}) collective-permute-start(bf16[2,2,256,256]{3,2,1,0:T(8,128)(2,1)} %param.9), channel_id=1, source_target_pairs={{0,2},{2,4},{4,6},{6,8},{8,10},{10,12},{12,14},{14,16},{16,18},{18... | collective-permute-start | bytes 1572872 | tf_op jit(solution)/shard_map/ppermute | solution.py:22
  8.6 197.8 %collective-permute-start.15 = (bf16[2,2,256,256]{3,2,1,0:T(8,128)(2,1)}, bf16[2,2,256,256]{3,2,1,0:T(8,128)(2,1)}, u32[]{:S(2)}, u32[]{:S(2)}) collective-permute-start(bf16[2,2,256,256]{3,2,1,0:T(8,128)(2,1)} %param.9), channel_id=1, source_target_pairs={{0,254},{2,0},{4,2},{6,4},{8,6},{10,8},{12,10},{14,12},{16,14},{18... | collective-permute-start | bytes 1572872 | tf_op jit(solution)/shard_map/ppermute | solution.py:22
  19.4 177.1 %collective-permute-start.10 = (bf16[2,2,64,512]{3,2,1,0:T(8,128)(2,1)}, bf16[2,2,64,512]{3,2,1,0:T(8,128)(2,1)}, u32[]{:S(2)}, u32[]{:S(2)}) collective-permute-start(bf16[2,2,64,512]{3,2,1,0:T(8,128)(2,1)} %param.10), channel_id=1, source_target_pairs={{0,2},{2,4},{4,6},{6,8},{8,10},{10,12},{12,14},{14,16},{16,18},{18... | collective-permute-start | bytes 786440 | tf_op jit(solution)/shard_map/ppermute | solution.py:22
  21.3 177.3 %collective-permute-start.16 = (bf16[2,2,64,512]{3,2,1,0:T(8,128)(2,1)}, bf16[2,2,64,512]{3,2,1,0:T(8,128)(2,1)}, u32[]{:S(2)}, u32[]{:S(2)}) collective-permute-start(bf16[2,2,64,512]{3,2,1,0:T(8,128)(2,1)} %param.10), channel_id=1, source_target_pairs={{0,254},{2,0},{4,2},{6,4},{8,6},{10,8},{12,10},{14,12},{16,14},{18... | collective-permute-start | bytes 786440 | tf_op jit(solution)/shard_map/ppermute | solution.py:22
  28.1 41.5 %collective-permute-start = (bf16[2,2,2,64,256]{4,3,0,2,1:T(8,128)(2,1)S(1)}, bf16[2,2,2,64,256]{4,3,0,2,1:T(8,128)(2,1)S(1)}, u32[]{:S(2)}, u32[]{:S(2)}) collective-permute-start(bf16[2,2,2,64,256]{4,3,0,2,1:T(8,128)(2,1)S(1)} %bitcast.655), channel_id=1, source_target_pairs={{0,256},{256,0},{1,257},{257,1},{2,258},{258,2},{3,259},{259,3},{4... | collective-permute-start | bytes 786440 | tf_op jit(solution)/shard_map/ppermute | solution.py:17
  69.7 4.1 collective-permute-start.1
  73.8 10.7 %collective-permute-start.2 = (bf16[2,2,2,64,256]{4,3,0,2,1:T(8,128)(2,1)S(1)}, bf16[2,2,2,64,256]{4,3,0,2,1:T(8,128)(2,1)S(1)}, u32[]{:S(2)}, u32[]{:S(2)}) collective-permute-start(bf16[2,2,2,64,256]{4,3,0,2,1:T(8,128)(2,1)S(1)} %collective-permute-done.1), channel_id=1, source_target_pairs={{0,4},{4,0},{2,6},{6,2},{8,12},{12,8},{10,14},{14,10},{16,20},{20,... | collective-permute-start | bytes 786440 | tf_op jit(solution)/shard_map/ppermute | solution.py:17
  84.5 16.3 %collective-permute-start.3 = (bf16[2,2,2,64,256]{4,3,0,2,1:T(8,128)(2,1)S(1)}, bf16[2,2,2,64,256]{4,3,0,2,1:T(8,128)(2,1)S(1)}, u32[]{:S(2)}, u32[]{:S(2)}) collective-permute-start(bf16[2,2,2,64,256]{4,3,0,2,1:T(8,128)(2,1)S(1)} %collective-permute-done.2), channel_id=1, source_target_pairs={{0,8},{8,0},{2,10},{10,2},{4,12},{12,4},{6,14},{14,6},{16,24},{24,... | collective-permute-start | bytes 786440 | tf_op jit(solution)/shard_map/ppermute | solution.py:17
  100.7 27.1 %collective-permute-start.4 = (bf16[2,2,2,64,256]{4,3,0,2,1:T(8,128)(2,1)S(1)}, bf16[2,2,2,64,256]{4,3,0,2,1:T(8,128)(2,1)S(1)}, u32[]{:S(2)}, u32[]{:S(2)}) collective-permute-start(bf16[2,2,2,64,256]{4,3,0,2,1:T(8,128)(2,1)S(1)} %collective-permute-done.3), channel_id=1, source_target_pairs={{0,16},{16,0},{2,18},{18,2},{4,20},{20,4},{6,22},{22,6},{8,24},{24... | collective-permute-start | bytes 786440 | tf_op jit(solution)/shard_map/ppermute | solution.py:17
  127.9 31.7 %collective-permute-start.5 = (bf16[2,2,2,64,256]{4,3,0,2,1:T(8,128)(2,1)S(1)}, bf16[2,2,2,64,256]{4,3,0,2,1:T(8,128)(2,1)S(1)}, u32[]{:S(2)}, u32[]{:S(2)}) collective-permute-start(bf16[2,2,2,64,256]{4,3,0,2,1:T(8,128)(2,1)S(1)} %collective-permute-done.4), channel_id=1, source_target_pairs={{0,32},{32,0},{2,34},{34,2},{4,36},{36,4},{6,38},{38,6},{8,40},{40... | collective-permute-start | bytes 786440 | tf_op jit(solution)/shard_map/ppermute | solution.py:17
  159.6 10.2 %collective-permute-start.6 = (bf16[2,2,2,64,256]{4,3,0,2,1:T(8,128)(2,1)S(1)}, bf16[2,2,2,64,256]{4,3,0,2,1:T(8,128)(2,1)}, u32[]{:S(2)}, u32[]{:S(2)}) collective-permute-start(bf16[2,2,2,64,256]{4,3,0,2,1:T(8,128)(2,1)S(1)} %collective-permute-done.5), channel_id=1, source_target_pairs={{0,64},{64,0},{2,66},{66,2},{4,68},{68,4},{6,70},{70,6},{8,72},{72... | collective-permute-start | bytes 786440 | tf_op jit(solution)/shard_map/ppermute | solution.py:17
  169.8 42.4 %collective-permute-start.7 = (bf16[2,2,2,64,256]{4,3,0,2,1:T(8,128)(2,1)}, bf16[2,2,2,64,256]{4,3,0,2,1:T(8,128)(2,1)}, u32[]{:S(2)}, u32[]{:S(2)}) collective-permute-start(bf16[2,2,2,64,256]{4,3,0,2,1:T(8,128)(2,1)} %collective-permute-done.6), channel_id=1, source_target_pairs={{0,128},{128,0},{2,130},{130,2},{4,132},{132,4},{6,134},{134,6},{8... | collective-permute-start | bytes 786440 | tf_op jit(solution)/shard_map/ppermute | solution.py:17
  196.6 293.5 %collective-permute-start.13 = (bf16[2,2,64,512]{3,2,1,0:T(8,128)(2,1)}, bf16[2,2,64,512]{3,2,1,0:T(8,128)(2,1)}, u32[]{:S(2)}, u32[]{:S(2)}) collective-permute-start(bf16[2,2,64,512]{3,2,1,0:T(8,128)(2,1)} %collective-permute-done.10), channel_id=1, source_target_pairs={{0,2},{2,4},{4,6},{6,8},{8,10},{10,12},{12,14},{14,16},{16,18},{18... | collective-permute-start | bytes 786440 | tf_op jit(solution)/shard_map/ppermute | solution.py:22
  198.6 303.9 %collective-permute-start.19 = (bf16[2,2,64,512]{3,2,1,0:T(8,128)(2,1)}, bf16[2,2,64,512]{3,2,1,0:T(8,128)(2,1)}, u32[]{:S(2)}, u32[]{:S(2)}) collective-permute-start(bf16[2,2,64,512]{3,2,1,0:T(8,128)(2,1)} %collective-permute-done.16), channel_id=1, source_target_pairs={{0,254},{2,0},{4,2},{6,4},{8,6},{10,8},{12,10},{14,12},{16,14},{18... | collective-permute-start | bytes 786440 | tf_op jit(solution)/shard_map/ppermute | solution.py:22
  204.4 275.8 %collective-permute-start.12 = (bf16[2,2,256,256]{3,2,1,0:T(8,128)(2,1)}, bf16[2,2,256,256]{3,2,1,0:T(8,128)(2,1)}, u32[]{:S(2)}, u32[]{:S(2)}) collective-permute-start(bf16[2,2,256,256]{3,2,1,0:T(8,128)(2,1)} %collective-permute-done.9), channel_id=1, source_target_pairs={{0,2},{2,4},{4,6},{6,8},{8,10},{10,12},{12,14},{14,16},{16,18},{18... | collective-permute-start | bytes 1572872 | tf_op jit(solution)/shard_map/ppermute | solution.py:22
  206.4 291.5 %collective-permute-start.18 = (bf16[2,2,256,256]{3,2,1,0:T(8,128)(2,1)}, bf16[2,2,256,256]{3,2,1,0:T(8,128)(2,1)}, u32[]{:S(2)}, u32[]{:S(2)}) collective-permute-start(bf16[2,2,256,256]{3,2,1,0:T(8,128)(2,1)} %collective-permute-done.15), channel_id=1, source_target_pairs={{0,254},{2,0},{4,2},{6,4},{8,6},{10,8},{12,10},{14,12},{16,14},{18... | collective-permute-start | bytes 1572872 | tf_op jit(solution)/shard_map/ppermute | solution.py:22
  216.3 234.2 %collective-permute-start.8 = (bf16[2,2,2,64,256]{4,3,0,2,1:T(8,128)(2,1)}, bf16[2,2,2,64,256]{4,3,0,2,1:T(8,128)(2,1)}, u32[]{:S(2)}, u32[]{:S(2)}) collective-permute-start(bf16[2,2,2,64,256]{4,3,0,2,1:T(8,128)(2,1)} %fusion.89), channel_id=1, source_target_pairs={{0,2},{2,4},{4,6},{6,8},{8,10},{10,12},{12,14},{14,16},{16,18},{18... | collective-permute-start | bytes 786440 | tf_op jit(solution)/shard_map/ppermute | solution.py:22
  223.5 224.2 %copy-start.46 = (bf16[2,2,64,256]{3,2,1,0:T(8,128)(2,1)S(1)}, bf16[2,2,64,256]{3,2,1,0:T(8,128)(2,1)}, u32[]{:S(2)}) copy-start(bf16[2,2,64,256]{3,2,1,0:T(8,128)(2,1)} %get-tuple-element.68) | copy-start | bytes 393220
  450.5 14.6 %collective-permute-start.14 = (bf16[2,2,2,64,256]{4,3,0,2,1:T(8,128)(2,1)}, bf16[2,2,2,64,256]{4,3,0,2,1:T(8,128)(2,1)S(1)}, u32[]{:S(2)}, u32[]{:S(2)}) collective-permute-start(bf16[2,2,2,64,256]{4,3,0,2,1:T(8,128)(2,1)} %fusion.89), channel_id=1, source_target_pairs={{0,254},{2,0},{4,2},{6,4},{8,6},{10,8},{12,10},{14,12},{16,14},{18... | collective-permute-start | bytes 786440 | tf_op jit(solution)/shard_map/ppermute | solution.py:22
  465.1 20.3 %collective-permute-start.11 = (bf16[2,2,2,64,256]{4,3,0,2,1:T(8,128)(2,1)}, bf16[2,2,2,64,256]{4,3,0,2,1:T(8,128)(2,1)S(1)}, u32[]{:S(2)}, u32[]{:S(2)}) collective-permute-start(bf16[2,2,2,64,256]{4,3,0,2,1:T(8,128)(2,1)} %collective-permute-done.8), channel_id=1, source_target_pairs={{0,2},{2,4},{4,6},{6,8},{8,10},{10,12},{12,14},{14,16},{16,18},{18... | collective-permute-start | bytes 786440 | tf_op jit(solution)/shard_map/ppermute | solution.py:22
  480.2 17.6 %collective-permute-start.17 = (bf16[2,2,2,64,256]{4,3,0,2,1:T(8,128)(2,1)S(1)}, bf16[2,2,2,64,256]{4,3,0,2,1:T(8,128)(2,1)S(1)}, u32[]{:S(2)}, u32[]{:S(2)}) collective-permute-start(bf16[2,2,2,64,256]{4,3,0,2,1:T(8,128)(2,1)S(1)} %collective-permute-done.14), channel_id=1, source_target_pairs={{0,254},{2,0},{4,2},{6,4},{8,6},{10,8},{12,10},{14,12},{16,14},{18... | collective-permute-start | bytes 786440 | tf_op jit(solution)/shard_map/ppermute | solution.py:22
  534.8 147.5 %copy-start.1 = (f32[512,256]{1,0:T(8,128)S(1)}, f32[512,256]{1,0:T(8,128)}, u32[]{:S(2)}) copy-start(f32[512,256]{1,0:T(8,128)} %param.13) | copy-start | bytes 1572868
  596.5 7.1 %collective-permute-start.20 = (bf16[2,2,2,64,128]{4,3,0,2,1:T(8,128)(2,1)S(1)}, bf16[2,2,2,64,128]{4,3,0,2,1:T(8,128)(2,1)S(1)}, u32[]{:S(2)}, u32[]{:S(2)}) collective-permute-start(bf16[2,2,2,64,128]{4,3,0,2,1:T(8,128)(2,1)S(1)} %add_convert_fusion.7), channel_id=1, source_target_pairs={{0,256},{256,0},{1,257},{257,1},{2,258},{258,2},{3,259},{259,3},{4... | collective-permute-start | bytes 393224 | tf_op jit(solution)/shard_map/ppermute | solution.py:17
  603.7 3.2 collective-permute-start.21
  606.9 7.4 %collective-permute-start.22 = (bf16[2,2,2,64,128]{4,3,0,2,1:T(8,128)(2,1)S(1)}, bf16[2,2,2,64,128]{4,3,0,2,1:T(8,128)(2,1)S(1)}, u32[]{:S(2)}, u32[]{:S(2)}) collective-permute-start(bf16[2,2,2,64,128]{4,3,0,2,1:T(8,128)(2,1)S(1)} %collective-permute-done.21), channel_id=1, source_target_pairs={{0,4},{4,0},{2,6},{6,2},{8,12},{12,8},{10,14},{14,10},{16,20},{20,... | collective-permute-start | bytes 393224 | tf_op jit(solution)/shard_map/ppermute | solution.py:17
  614.4 10.3 %collective-permute-start.23 = (bf16[2,2,2,64,128]{4,3,0,2,1:T(8,128)(2,1)S(1)}, bf16[2,2,2,64,128]{4,3,0,2,1:T(8,128)(2,1)S(1)}, u32[]{:S(2)}, u32[]{:S(2)}) collective-permute-start(bf16[2,2,2,64,128]{4,3,0,2,1:T(8,128)(2,1)S(1)} %collective-permute-done.22), channel_id=1, source_target_pairs={{0,8},{8,0},{2,10},{10,2},{4,12},{12,4},{6,14},{14,6},{16,24},{24,... | collective-permute-start | bytes 393224 | tf_op jit(solution)/shard_map/ppermute | solution.py:17
  624.7 17.5 %collective-permute-start.24 = (bf16[2,2,2,64,128]{4,3,0,2,1:T(8,128)(2,1)S(1)}, bf16[2,2,2,64,128]{4,3,0,2,1:T(8,128)(2,1)S(1)}, u32[]{:S(2)}, u32[]{:S(2)}) collective-permute-start(bf16[2,2,2,64,128]{4,3,0,2,1:T(8,128)(2,1)S(1)} %collective-permute-done.23), channel_id=1, source_target_pairs={{0,16},{16,0},{2,18},{18,2},{4,20},{20,4},{6,22},{22,6},{8,24},{24... | collective-permute-start | bytes 393224 | tf_op jit(solution)/shard_map/ppermute | solution.py:17
  642.2 24.1 %collective-permute-start.25 = (bf16[2,2,2,64,128]{4,3,0,2,1:T(8,128)(2,1)S(1)}, bf16[2,2,2,64,128]{4,3,0,2,1:T(8,128)(2,1)S(1)}, u32[]{:S(2)}, u32[]{:S(2)}) collective-permute-start(bf16[2,2,2,64,128]{4,3,0,2,1:T(8,128)(2,1)S(1)} %collective-permute-done.24), channel_id=1, source_target_pairs={{0,32},{32,0},{2,34},{34,2},{4,36},{36,4},{6,38},{38,6},{8,40},{40... | collective-permute-start | bytes 393224 | tf_op jit(solution)/shard_map/ppermute | solution.py:17
  666.3 6.8 collective-permute-start.26
  673.2 8.4 %collective-permute-start.27 = (bf16[2,2,2,64,128]{4,3,0,2,1:T(8,128)(2,1)S(1)}, bf16[2,2,2,64,128]{4,3,0,2,1:T(8,128)(2,1)S(1)}, u32[]{:S(2)}, u32[]{:S(2)}) collective-permute-start(bf16[2,2,2,64,128]{4,3,0,2,1:T(8,128)(2,1)S(1)} %collective-permute-done.26), channel_id=1, source_target_pairs={{0,128},{128,0},{2,130},{130,2},{4,132},{132,4},{6,134},{134,6},{8... | collective-permute-start | bytes 393224 | tf_op jit(solution)/shard_map/ppermute | solution.py:17
  (58 other events, 541.6 us)
Sparse Core Ops, SparseCore 0:
  536.4 57.7 reduce-scatter.3
